TPU v7x, 512 devices: a whole 4x8x8 slice. The times are simulated.
512 devices in a mesh: chan: 8 (over x, core), row: 8 (over z), col: 8 (over y).
Axes of the slice: x: 4, y: 8, z: 8, core: 2. Of those that a mesh axis runs over, the one named last changes fastest.
Arguments:
- visibility: bfloat16 [64, 1, 2, 2048, 2048], P('chan', None, None, 'row', 'col'), parts along dimension 0
- model: bfloat16 [64, 1, 2, 2048, 2048], P('chan', None, None, 'row', 'col'), parts along dimension 0
- gains_init: float32 [64, 1, 2, 2048], P('chan'), parts along dimension 0, may hold values from 0.1 to 1.9
- antenna_mask: int32 [64, 2048], P('chan'), parts along dimension 0, may hold values 0 or 1
Outputs:
- gains: float32 [64, 1, 2, 2048], P('chan', None, None, 'row'), parts along dimension 0
There are 8 independent parts, one for each index of `chan`. A program takes and returns all parts, laid end to end along the dimension named above; each array names one. Nothing has to cross between parts.
All inputs are finite; a program needn't handle non-finite values.
Results may differ from a plain program's by a relative error of at most 0.0003.
Values sent between devices are 32-bit elements; how exact they have to be, the bound alone decides.
A program may use at most 64 MiB of HBM per device.

v0:
```python
import jax
import jax.numpy as jnp
from jax import lax
from jax.sharding import PartitionSpec as P

ITERS = 3


def update_gains(num_re, num_im, den, mask_piece, old, step):
    scale = mask_piece[:, None, :] / jnp.maximum(den, 1.0)
    keep = 1.0 - mask_piece[:, None, :]
    new_re = num_re * scale + keep * old[:, :, 0]
    new_im = num_im * scale + keep * old[:, :, 1]
    fresh = jnp.stack([new_re, new_im], axis=2)
    if step % 2 == 1:
        return 0.5 * (fresh + old)
    return fresh


def per_device(visibility, model, gains_init, antenna_mask):
    rows_n = visibility.shape[3]
    cols_n = visibility.shape[4]
    total = gains_init.shape[3]
    row_start = lax.axis_index("row") * rows_n
    col_start = lax.axis_index("col") * cols_n
    mask_f = antenna_mask.astype(jnp.float32)
    row_mask = lax.dynamic_slice_in_dim(mask_f, row_start, rows_n, 1)
    col_mask = lax.dynamic_slice_in_dim(mask_f, col_start, cols_n, 1)
    row_ids = row_start + lax.iota(jnp.int32, rows_n)
    col_ids = col_start + lax.iota(jnp.int32, cols_n)
    off_diag = (row_ids[:, None] != col_ids[None, :]).astype(jnp.float32)
    weight = (row_mask[:, :, None] * col_mask[:, None, :] * off_diag[None])[:, None]
    vis_re = visibility[:, :, 0]
    vis_im = visibility[:, :, 1]
    mod_re = model[:, :, 0]
    mod_im = model[:, :, 1]
    gains = gains_init
    for step in range(ITERS):
        col_gains = lax.dynamic_slice_in_dim(gains, col_start, cols_n, 3)
        g_re = col_gains[:, :, 0][:, :, None, :]
        g_im = col_gains[:, :, 1][:, :, None, :]
        z_re = mod_re * g_re + mod_im * g_im
        z_im = mod_im * g_re - mod_re * g_im
        num_re = jnp.sum(weight * (z_re * vis_re + z_im * vis_im), axis=-1)
        num_im = jnp.sum(weight * (z_re * vis_im - z_im * vis_re), axis=-1)
        den = jnp.sum(weight * (z_re * z_re + z_im * z_im), axis=-1)
        blank = jnp.zeros(num_re.shape[:2] + (total,), jnp.float32)
        wide_re = lax.dynamic_update_slice_in_dim(blank, num_re, row_start, 2)
        wide_im = lax.dynamic_update_slice_in_dim(blank, num_im, row_start, 2)
        wide_den = lax.dynamic_update_slice_in_dim(blank, den, row_start, 2)
        sum_re, sum_im, sum_den = lax.psum((wide_re, wide_im, wide_den), ("row", "col"))
        gains = update_gains(sum_re, sum_im, sum_den, mask_f, gains, step)
    return lax.dynamic_slice_in_dim(gains, row_start, rows_n, 3)


def solution(mesh):
    return jax.shard_map(
        per_device,
        mesh=mesh,
        in_specs=(
            P("chan", None, None, "row", "col"),
            P("chan", None, None, "row", "col"),
            P("chan", None, None, None),
            P("chan", None),
        ),
        out_specs=P("chan", None, None, "row"),
        check_vma=False,
    )
```

profile of v0, /device:TPU:6, one launch (start us, length us, event | category | flops | bytes accessed | tf_op | source)
XLA Modules:
  0.0 489.0 jit_solution(2505661483002709844)
XLA Ops:
  6.5 0.8 convert_element_type.190
  7.4 0.9 constant_dynamic-slice_fusion
  8.3 0.1 compare_convert_fusion
  8.4 0.0 copy-start.14
  8.4 0.0 copy-start.1
  8.4 4.5 fusion.8
  13.1 0.5 copy-done.3
  13.6 0.0 copy-done.4
  13.7 0.1 copy-done.5
  13.7 0.0 all-reduce.11.cloned.1.call-update
  13.7 0.0 all-reduce.9.cloned.1.call-start
  13.8 0.1 fusion.47
  13.9 157.1 %all-reduce.11.cloned.1.call-done = (f32[8,1,2048]{2,0,1:T(8,128)}, f32[8,1,2048]{2,0,1:T(8,128)}, f32[8,1,2048]{2,0,1:T(8,128)}) async-done(((f32[8,1,2048]{2,0,1:T(8,128)}, f32[8,1,2048]{2,0,1:T(8,128)}, f32[8,1,2048]{2,0,1:T(8,128)}), (f32[8,1,2048]{2,0,1:T(8,128)}, f32[8,1,2048]{2,0,1:T(8,128)}, f32[8,1,2048]{2,0,1:T(8,128)})) %all-reduce.11.cloned.1.call-update) | async-done | bytes 196624 | tf_op jit(solution)/shard_map/psum | solution.py:51
  171.0 1.0 fusion.45
  172.1 4.1 fusion.14
  176.3 0.5 copy-done.6
  176.8 0.0 copy-done.7
  176.9 0.0 copy-done.8
  176.9 0.0 all-reduce.9.cloned.1.call-update
  177.0 0.0 all-reduce.7.cloned.1.call-start
  177.0 148.8 %all-reduce.9.cloned.1.call-done = (f32[8,1,2048]{2,0,1:T(8,128)}, f32[8,1,2048]{2,0,1:T(8,128)}, f32[8,1,2048]{2,0,1:T(8,128)}) async-done(((f32[8,1,2048]{2,0,1:T(8,128)}, f32[8,1,2048]{2,0,1:T(8,128)}, f32[8,1,2048]{2,0,1:T(8,128)}), (f32[8,1,2048]{2,0,1:T(8,128)}, f32[8,1,2048]{2,0,1:T(8,128)}, f32[8,1,2048]{2,0,1:T(8,128)})) %all-reduce.9.cloned.1.call-update) | async-done | bytes 196624 | tf_op jit(solution)/shard_map/psum | solution.py:51
  325.9 1.0 fusion.38
  326.9 4.1 fusion.23
  331.1 0.5 copy-done.9
  331.6 0.0 copy-done.10
  331.7 0.1 copy-done.2
  331.7 0.0 all-reduce.7.cloned.1.call-update
  331.8 148.9 %all-reduce.7.cloned.1.call-done = (f32[8,1,2048]{2,0,1:T(8,128)}, f32[8,1,2048]{2,0,1:T(8,128)}, f32[8,1,2048]{2,0,1:T(8,128)}) async-done(((f32[8,1,2048]{2,0,1:T(8,128)}, f32[8,1,2048]{2,0,1:T(8,128)}, f32[8,1,2048]{2,0,1:T(8,128)}), (f32[8,1,2048]{2,0,1:T(8,128)}, f32[8,1,2048]{2,0,1:T(8,128)}, f32[8,1,2048]{2,0,1:T(8,128)})) %all-reduce.7.cloned.1.call-update) | async-done | bytes 196624 | tf_op jit(solution)/shard_map/psum | solution.py:51
  480.7 0.9 fusion.42
  481.6 0.1 copy.19
  481.7 0.1 fusion.41
  481.8 0.7 fusion.43
  (46 shorter events, 0.2 us)
Async XLA Ops:
  6.5 164.5 %all-reduce.11.cloned.1.call-start = ((), (), s32[]{:S(2)}) async-start(), calls=%async_computation.2 | async-start | bytes 393216 | tf_op jit(solution)/shard_map/psum | solution.py:51
  8.4 5.4 %copy-start.14 = (f32[8,1,2,2048]{3,2,1,0:T(2,128)S(1)}, f32[8,1,2,2048]{3,2,1,0:T(2,128)}, u32[]{:S(2)}) copy-start(f32[8,1,2,2048]{3,2,1,0:T(2,128)} %param.6) | copy-start | bytes 393220
  8.4 162.6 %copy-start.1 = (s32[8,2048]{1,0:T(8,128)S(1)}, s32[8,2048]{1,0:T(8,128)}, u32[]{:S(2)}) copy-start(s32[8,2048]{1,0:T(8,128)} %param.7) | copy-start | bytes 196612
  8.4 163.6 %copy-start = (bf16[8,1,2,256,256]{4,3,2,1,0:T(8,128)(2,1)S(1)}, bf16[8,1,2,256,256]{4,3,2,1,0:T(8,128)(2,1)}, u32[]{:S(2)}) copy-start(bf16[8,1,2,256,256]{4,3,2,1,0:T(8,128)(2,1)} %param.4) | copy-start | bytes 6291460
  13.0 0.6 copy-start.3
  13.0 0.6 copy-start.4
  13.1 0.6 copy-start.5
  13.7 312.1 %all-reduce.9.cloned.1.call-start = ((), (), s32[]{:S(2)}) async-start(), calls=%async_computation.1 | async-start | bytes 393216 | tf_op jit(solution)/shard_map/psum | solution.py:51
  172.0 153.8 %copy-start.11 = (f32[8,1,2048]{2,0,1:T(8,128)S(1)}, f32[8,1,2048]{2,0,1:T(8,128)}, u32[]{:S(2)}) copy-start(f32[8,1,2048]{2,0,1:T(8,128)} %get-tuple-element.20) | copy-start | bytes 196612
  172.1 153.8 %copy-start.12 = (f32[8,1,2048]{2,0,1:T(8,128)S(1)}, f32[8,1,2048]{2,0,1:T(8,128)}, u32[]{:S(2)}) copy-start(f32[8,1,2048]{2,0,1:T(8,128)} %get-tuple-element.21) | copy-start | bytes 196612
  172.1 153.8 %copy-start.13 = (f32[8,1,2048]{2,0,1:T(8,128)S(1)}, f32[8,1,2048]{2,0,1:T(8,128)}, u32[]{:S(2)}) copy-start(f32[8,1,2048]{2,0,1:T(8,128)} %get-tuple-element.22) | copy-start | bytes 196612
  176.2 0.6 copy-start.6
  176.3 0.6 copy-start.7
  176.3 0.6 copy-start.8
  177.0 303.7 %all-reduce.7.cloned.1.call-start = ((), (), s32[]{:S(2)}) async-start(), calls=%async_computation | async-start | bytes 393216 | tf_op jit(solution)/shard_map/psum | solution.py:51
  331.0 0.6 copy-start.9
  331.1 0.6 copy-start.10
  331.1 0.6 copy-start.2
Sparse Core Ops, SparseCore 0:
  13.9 157.1 all-reduce.10
  177.1 148.7 all-reduce.8
  331.9 148.7 all-reduce.6
where the time goes:
time: 489 us
  waiting for transfers between devices  455 us (93%)
  other arithmetic  17.4 us (4%)
  between operations  13.5 us (3%)
    psum x3, waiting for transfers between devices, per_device(): lax.psum((wide_re, wide_im, wide_den), ('row', 'col'))  455 us
  transfers between devices with their start and end apart: 3, of which 3 were waited for; matrix products, arithmetic and copies ran while one was open for 0% of the time, Pallas kernels for 0%

commit v1 on v0

v1 whole, which is shorter than its diff:
```python
import functools

import jax
import jax.numpy as jnp
from jax import lax
from jax.experimental import pallas as pl
from jax.experimental.pallas import tpu as pltpu
from jax.sharding import PartitionSpec as P

ITERS = 3
MESH = pl.DeviceIdType.MESH
SHRINK = 2.0**-8
HUGE = 2.0**60
HUGE_SHRINK = 2.0**-65
LOWER = 2.0**-4
HUGE_GROW = 2.0**126
LEAST = SHRINK * LOWER
CHUNK = 32


def split(x):
    high = x.astype(jnp.bfloat16).astype(jnp.float32)
    return high, x - high


def stack_bf16(parts):
    return jnp.concatenate(parts, axis=0).astype(jnp.bfloat16)


def dot_nt(x, y):
    return lax.dot_general(x, y, (((1,), (1,)), ((), ())), preferred_element_type=jnp.float32)


def kernel(
    n, vis, mod, gin, mask, out,
    vbuf, mbuf, abuf, bbuf, weight, gcol, gown, mcol, mrow,
    part, recv, gsend, xbuf,
    in_sem, small_sem, send1, recv1, send2, recv2, send3, recv3, self_sem,
):
    row = lax.axis_index("row")
    col = lax.axis_index("col")
    wide = weight.shape[1]
    diag = row == col

    def loads(k):
        return (
            pltpu.make_async_copy(vis.at[k], vbuf.at[k], in_sem.at[0, k]),
            pltpu.make_async_copy(mod.at[k], mbuf.at[k], in_sem.at[1, k]),
        )

    row_at = pl.ds(pl.multiple_of(row * wide, wide), wide)
    col_at = pl.ds(pl.multiple_of(col * wide, wide), wide)
    small = (
        pltpu.make_async_copy(gin.at[:, :, col_at], gcol, small_sem.at[0]),
        pltpu.make_async_copy(mask.at[:, col_at], mcol, small_sem.at[1]),
        pltpu.make_async_copy(mask.at[:, row_at], mrow, small_sem.at[2]),
        pltpu.make_async_copy(gin.at[col, :, row_at], gown, small_sem.at[3]),
    )
    for step in range(1, n + 1):
        for copy in loads(lax.rem(col + step, n)):
            copy.start()
        if step == 1:
            for copy in small:
                copy.start()

    barrier = pltpu.get_barrier_semaphore()
    for step in range(1, n):
        pl.semaphore_signal(barrier, inc=1, device_id={"col": lax.rem(col + step, n)}, device_id_type=MESH)
    for step in range(n):
        peer = {"row": col, "col": lax.rem(col + step, n)}
        if step == 0:
            @pl.when(jnp.logical_not(diag))
            def _():
                pl.semaphore_signal(barrier, inc=1, device_id=peer, device_id_type=MESH)
        else:
            pl.semaphore_signal(barrier, inc=1, device_id=peer, device_id_type=MESH)

    row_ids = lax.broadcasted_iota(jnp.int32, weight.shape, 0) + row * wide
    col_ids = lax.broadcasted_iota(jnp.int32, weight.shape, 1) + col * wide
    weight[...] = jnp.where(row_ids == col_ids, 0.0, SHRINK)

    for copy in small:
        copy.wait()
    xbuf[0] = gcol[...] * mcol[...].astype(jnp.float32)[:, None, :]

    even = lax.rem(lax.broadcasted_iota(jnp.int32, (8, wide), 0), 2) == 0
    top = lax.broadcasted_iota(jnp.int32, (4, wide), 0) < 2

    def prepare(k):
        for copy in loads(k):
            copy.wait()
        for at in range(0, wide, CHUNK):
            rows = pl.ds(at, CHUNK)
            scale = weight[rows]
            m_re = mbuf[k, 0, rows].astype(jnp.float32)
            m_im = mbuf[k, 1, rows].astype(jnp.float32)
            v_re = vbuf[k, 0, rows].astype(jnp.float32)
            v_im = vbuf[k, 1, rows].astype(jnp.float32)
            s_re = m_re * scale
            s_im = m_im * scale
            for place, value in enumerate((s_re * v_re + s_im * v_im, s_re * v_im - s_im * v_re)):
                high = value.astype(jnp.bfloat16)
                abuf[k, rows, (2 * place) * wide:(2 * place + 1) * wide] = high
                abuf[k, rows, (2 * place + 1) * wide:(2 * place + 2) * wide] = (value - high.astype(jnp.float32)).astype(jnp.bfloat16)
            value = s_re * m_re + s_im * m_im
            high = value.astype(jnp.bfloat16)
            bbuf[k, rows, 0:wide] = high
            bbuf[k, rows, wide:2 * wide] = (value - high.astype(jnp.float32)).astype(jnp.bfloat16)

    def multiply(it, k):
        x_re = jnp.broadcast_to(xbuf[it, k, 0:1, :], (8, wide))
        x_im = jnp.broadcast_to(xbuf[it, k, 1:2, :], (8, wide))
        by_re = stack_bf16(split(jnp.where(even, x_re, x_im)))
        by_im = stack_bf16(split(jnp.where(even, -x_im, x_re)))
        huge = jnp.maximum(jnp.abs(x_re), jnp.abs(x_im)) > HUGE
        down = jnp.where(huge, HUGE_SHRINK, 1.0)
        square = (x_re * down) * (x_re * down) + (x_im * down) * (x_im * down)
        by_b = stack_bf16(split(jnp.where(huge, 0.0, square)) + split(jnp.where(huge, square, 0.0)))
        num = dot_nt(jnp.concatenate([by_re, by_re, by_im, by_im], axis=1), abuf[k])
        den = dot_nt(jnp.concatenate([by_b, by_b], axis=1), bbuf[k])
        num = (num[0:8] + num[8:16]) * LOWER
        den = (den[0:8] + den[8:16]) * LOWER + (den[16:24] + den[24:32]) * HUGE_GROW
        part[it, k] = jnp.where(top, num[0:4], den[0:4])

    def send_part(it, step):
        k = lax.rem(col + step, n)
        pltpu.make_async_remote_copy(
            src_ref=part.at[it, k], dst_ref=recv.at[it, step - 1],
            send_sem=send1.at[it], recv_sem=recv1.at[it],
            device_id={"col": k}, device_id_type=MESH,
        ).start()

    def wait_bytes(ref, sem):
        pltpu.make_async_copy(ref, ref, sem).wait()

    for it in range(ITERS):
        if it == 0:
            first = lax.rem(col + 1, n)
            prepare(first)
            multiply(0, first)
            pl.semaphore_wait(barrier, 2 * n - 1 - diag.astype(jnp.int32))
            send_part(0, 1)

            @pl.loop(2, n)
            def _(step):
                k = lax.rem(col + step, n)
                prepare(k)
                multiply(0, k)
                send_part(0, step)

            prepare(col)
            multiply(0, col)
        else:
            wait_bytes(xbuf.at[it], recv2.at[it - 1])

            @pl.loop(1, n)
            def _(step):
                multiply(it, lax.rem(col + step, n))
                send_part(it, step)

            multiply(it, col)

        wait_bytes(recv.at[it], recv1.at[it])
        total = part[it, col]
        for step in range(n - 1):
            total = total + recv[it, step]
        old = gown[...]
        own_mask = mrow[pl.ds(col, 1), :].astype(jnp.float32)
        fresh = total[0:2] / jnp.maximum(total[2:4], LEAST)
        fresh = jnp.where(own_mask > 0.0, fresh, old)
        if it % 2 == 1:
            fresh = 0.5 * (fresh + old)
        if it < ITERS - 1:
            gown[...] = fresh
            gsend[it] = fresh * own_mask
            for step in range(n):
                peer = {"row": lax.rem(row + step, n), "col": row}

                def remote(step=step, peer=peer):
                    pltpu.make_async_remote_copy(
                        src_ref=gsend.at[it], dst_ref=xbuf.at[it + 1, col],
                        send_sem=send2.at[it, min(step, 1)], recv_sem=recv2.at[it],
                        device_id=peer, device_id_type=MESH,
                    ).start()

                if step == 0:
                    pl.when(jnp.logical_not(diag))(remote)

                    @pl.when(diag)
                    def _():
                        pltpu.make_async_copy(gsend.at[it], xbuf.at[it + 1, col], recv2.at[it]).start()
                else:
                    remote()
        else:
            gsend[it] = fresh
            for step in range(1, n):
                pltpu.make_async_remote_copy(
                    src_ref=gsend.at[it], dst_ref=out.at[col],
                    send_sem=send3, recv_sem=recv3,
                    device_id={"col": lax.rem(col + step, n)}, device_id_type=MESH,
                ).start()
            own = pltpu.make_async_copy(gsend.at[it], out.at[col], self_sem)
            own.start()
            own.wait()

    for it in range(ITERS):
        wait_bytes(recv.at[it], send1.at[it])
        if it < ITERS - 1:
            wait_bytes(xbuf.at[it + 1, 0:n - 1], send2.at[it, 1])

            @pl.when(jnp.logical_not(diag))
            def _():
                wait_bytes(gsend.at[it], send2.at[it, 0])
    wait_bytes(xbuf.at[0, 0:n - 1], send3)
    wait_bytes(xbuf.at[0, 0:n - 1], recv3)


def per_device(n, visibility, model, gains_init, antenna_mask):
    ch, _, _, rows, wide = visibility.shape
    f32, bf16 = jnp.float32, jnp.bfloat16
    hbm = pl.BlockSpec(memory_space=pltpu.HBM)
    dma = pltpu.SemaphoreType.DMA
    gains = pl.pallas_call(
        functools.partial(kernel, n),
        out_shape=jax.ShapeDtypeStruct((ch, 2, wide), f32),
        in_specs=[hbm] * 4,
        out_specs=hbm,
        scratch_shapes=[
            pltpu.VMEM((ch, 2, rows, wide), bf16),
            pltpu.VMEM((ch, 2, rows, wide), bf16),
            pltpu.VMEM((ch, rows, 4 * wide), bf16),
            pltpu.VMEM((ch, rows, 2 * wide), bf16),
            pltpu.VMEM((rows, wide), f32),
            pltpu.VMEM((ch, 2, wide), f32),
            pltpu.VMEM((2, wide), f32),
            pltpu.VMEM((ch, wide), jnp.int32),
            pltpu.VMEM((ch, wide), jnp.int32),
            pltpu.VMEM((ITERS, ch, 4, wide), f32),
            pltpu.VMEM((ITERS, n - 1, 4, wide), f32),
            pltpu.VMEM((ITERS, 2, wide), f32),
            pltpu.VMEM((ITERS, ch, 2, wide), f32),
            dma((2, ch)),
            dma((4,)),
            dma((ITERS,)),
            dma((ITERS,)),
            dma((ITERS - 1, 2)),
            dma((ITERS - 1,)),
            dma,
            dma,
            dma,
        ],
        compiler_params=pltpu.CompilerParams(
            collective_id=0, has_side_effects=True, vmem_limit_bytes=60 * 2**20
        ),
        cost_estimate=pl.CostEstimate(flops=2 * 48 * 16 * 256 * 256 * 3, bytes_accessed=4 * 2**20, transcendentals=0),
    )(
        visibility.reshape(ch, 2, rows, wide),
        model.reshape(ch, 2, rows, wide),
        gains_init.reshape(ch, 2, gains_init.shape[3]),
        antenna_mask,
    )
    return gains.reshape(ch, 1, 2, wide)


def solution(mesh):
    n = mesh.shape["col"]
    assert mesh.shape["row"] == n
    return jax.shard_map(
        functools.partial(per_device, n),
        mesh=mesh,
        in_specs=(
            P("chan", None, None, "row", "col"),
            P("chan", None, None, "row", "col"),
            P("chan", None, None, None),
            P("chan", None),
        ),
        out_specs=P("chan", None, None, "row"),
        check_vma=False,
    )
```

time: 489 us -> 49.3 us (0.10)
  waiting for transfers between devices: 455 us -> 0 us
  Pallas kernels: 0 us -> 47.7 us
  other arithmetic: 17.4 us -> 0 us
  between operations: 13.5 us -> 0.01 us
    psum x3 -> x0, waiting for transfers between devices: 455 us -> none  [per_device(): lax.psum((wide_re, wide_im, wide_den), ('row', 'col'))]
    pallas_call x0 -> x1, Pallas kernels: none -> 47.7 us  [per_device(): pl.pallas_call(functools.partial(kernel, n), out_shape=jax.ShapeDtypeStru...]
    reduce_sum x3 -> x0, other arithmetic: 12.8 us -> none  [the longest x2 8.65 us: per_device(): num_re = jnp.sum(weight * (z_re * vis_re + z_im * vis_im), axis=-1)]
  transfers between devices with their start and end apart: 3 -> 0, of which waited for: 3 -> 0; matrix products, arithmetic and copies ran while one was open for 0% -> 0% of each run, Pallas kernels for 0% -> 0%
where the time goes in v1:
time: 49.3 us; the launch traced here: 49.1 us
  Pallas kernels  47.7 us (97%)
  local copies, waits for them, and re-layouts  1.32 us (3%)
    pallas_call x1, Pallas kernels, per_device(): pl.pallas_call(functools.partial(kernel, n), out_shape=jax.ShapeDtypeStru...  47.7 us
    unnamed x1, local copies, waits for them, and re-layouts  1.32 us

profile of v1, /device:TPU:6, one launch (start us, length us, event | category | flops | bytes accessed | tf_op | source)
XLA Modules:
  0.0 49.1 jit_solution(13442581335082272980)
XLA Ops:
  0.0 47.7 %shard_map.46 = f32[8,2,256]{2,1,0:T(2,128)} custom-call(bf16[8,2,256,256]{3,2,1,0:T(8,128)(2,1)} %bitcast.6, bf16[8,2,256,256]{3,2,1,0:T(8,128)(2,1)} %bitcast.7, f32[8,2,2048]{2,1,0:T(2,128)} %bitcast.8, s32[8,2048]{1,0:T(8,128)} %mask.1), custom_call_target="tpu_custom_call" | custom-call | flops 301989888 | bytes 4194304 | tf_op jit(solution)/shard_map/pallas_call | solution.py:223
  47.7 1.3 %copy.7 = f32[8,1,2,256]{3,2,1,0:T(2,128)} copy(f32[8,1,2,256]{3,2,1,0:T(2,128)} %bitcast.9) | data formatting | bytes 32768

commit v2 on v1

v2 whole, which is shorter than its diff:
```python
import functools

import jax
import jax.numpy as jnp
from jax import lax
from jax.experimental import pallas as pl
from jax.experimental.pallas import tpu as pltpu
from jax.sharding import PartitionSpec as P

ITERS = 3
MESH = pl.DeviceIdType.MESH
SHRINK = 2.0**-8
HUGE = 2.0**60
HUGE_SHRINK = 2.0**-65
LOWER = 2.0**-4
HUGE_GROW = 2.0**126
LEAST = SHRINK * LOWER
CHUNK = 32


def split(x):
    high = x.astype(jnp.bfloat16).astype(jnp.float32)
    return high, x - high


def stack_bf16(parts):
    return jnp.concatenate(parts, axis=0).astype(jnp.bfloat16)


def dot_nt(x, y):
    return lax.dot_general(x, y, (((1,), (1,)), ((), ())), preferred_element_type=jnp.float32)


def farthest_first(n):
    return sorted(range(1, n), key=lambda step: -min(step, n - step))


def kernel(
    n, vis, mod, gin, mask, out,
    vbuf, mbuf, abuf, bbuf, weight, gcol, grow, mcol, mrow, old, sums, xbuf, final,
    in_sem, small_sem, sum_send, sum_recv, x_send, x_recv, out_sem,
):
    row = lax.axis_index("row")
    col = lax.axis_index("col")
    ch, wide = mcol.shape
    diag = row == col

    def loads(k):
        return (
            pltpu.make_async_copy(vis.at[k], vbuf.at[k], in_sem.at[0, k]),
            pltpu.make_async_copy(mod.at[k], mbuf.at[k], in_sem.at[1, k]),
        )

    row_at = pl.ds(pl.multiple_of(row * wide, wide), wide)
    col_at = pl.ds(pl.multiple_of(col * wide, wide), wide)
    small = (
        pltpu.make_async_copy(gin.at[:, :, col_at], gcol, small_sem.at[0]),
        pltpu.make_async_copy(mask.at[:, col_at], mcol, small_sem.at[1]),
        pltpu.make_async_copy(mask.at[:, row_at], mrow, small_sem.at[2]),
        pltpu.make_async_copy(gin.at[:, :, row_at], grow, small_sem.at[3]),
    )
    for k in range(ch):
        for copy in loads(k):
            copy.start()
        if k == 0:
            for copy in small:
                copy.start()

    barrier = pltpu.get_barrier_semaphore()
    for step in range(1, n):
        pl.semaphore_signal(barrier, inc=1, device_id={"col": lax.rem(col + step, n)}, device_id_type=MESH)

    @pl.when(jnp.logical_not(diag))
    def _():
        pl.semaphore_signal(barrier, inc=1, device_id={"row": col}, device_id_type=MESH)

    row_ids = lax.broadcasted_iota(jnp.int32, weight.shape, 0) + row * wide
    col_ids = lax.broadcasted_iota(jnp.int32, weight.shape, 1) + col * wide
    weight[...] = jnp.where(row_ids == col_ids, 0.0, SHRINK)

    for copy in small:
        copy.wait()
    col_mask = mcol[...].astype(jnp.float32)
    for part in range(2):
        xbuf[0, part] = gcol[:, part, :] * col_mask
        old[part] = grow[:, part, :]

    channel = lax.broadcasted_iota(jnp.int32, (ch, wide), 0)

    def prepare(k):
        for copy in loads(k):
            copy.wait()
        for at in range(0, wide, CHUNK):
            rows = pl.ds(at, CHUNK)
            scale = weight[rows]
            m_re = mbuf[k, 0, rows].astype(jnp.float32)
            m_im = mbuf[k, 1, rows].astype(jnp.float32)
            v_re = vbuf[k, 0, rows].astype(jnp.float32)
            v_im = vbuf[k, 1, rows].astype(jnp.float32)
            s_re = m_re * scale
            s_im = m_im * scale
            for place, value in enumerate((s_re * v_re + s_im * v_im, s_re * v_im - s_im * v_re)):
                high = value.astype(jnp.bfloat16)
                abuf[k, rows, (2 * place) * wide:(2 * place + 1) * wide] = high
                abuf[k, rows, (2 * place + 1) * wide:(2 * place + 2) * wide] = (value - high.astype(jnp.float32)).astype(jnp.bfloat16)
            value = s_re * m_re + s_im * m_im
            high = value.astype(jnp.bfloat16)
            bbuf[k, rows, 0:wide] = high
            bbuf[k, rows, wide:2 * wide] = (value - high.astype(jnp.float32)).astype(jnp.bfloat16)

    def multiply(it):
        x_re = xbuf[it, 0]
        x_im = xbuf[it, 1]
        re = split(x_re)
        im = split(x_im)
        by_re = stack_bf16(re + im)
        by_im = stack_bf16((-im[0], -im[1]) + re)
        huge = jnp.maximum(jnp.abs(x_re), jnp.abs(x_im)) > HUGE
        down = jnp.where(huge, HUGE_SHRINK, 1.0)
        square = (x_re * down) * (x_re * down) + (x_im * down) * (x_im * down)
        by_b = stack_bf16(split(jnp.where(huge, 0.0, square)) + split(jnp.where(huge, square, 0.0)))
        by_a = jnp.concatenate([by_re, by_re, by_im, by_im], axis=1)
        by_b = jnp.concatenate([by_b, by_b], axis=1)
        num_re = num_im = den = jnp.zeros((ch, wide), jnp.float32)
        for k in range(ch):
            num = dot_nt(by_a, abuf[k])
            sq = dot_nt(by_b, bbuf[k])
            here = channel == k
            num_re = jnp.where(here, num[0:ch] + num[ch:2 * ch], num_re)
            num_im = jnp.where(here, num[2 * ch:3 * ch] + num[3 * ch:4 * ch], num_im)
            den = jnp.where(here, (sq[0:ch] + sq[ch:2 * ch]) * LOWER + (sq[2 * ch:3 * ch] + sq[3 * ch:4 * ch]) * HUGE_GROW, den)
        sums[it, col, 0] = num_re * LOWER
        sums[it, col, 1] = num_im * LOWER
        sums[it, col, 2] = den

    def sum_to(it, peer):
        return pltpu.make_async_remote_copy(
            src_ref=sums.at[it, col], dst_ref=sums.at[it, col],
            send_sem=sum_send.at[it], recv_sem=sum_recv.at[it],
            device_id={"col": peer}, device_id_type=MESH,
        )

    def wait_bytes(ref, sem):
        pltpu.make_async_copy(ref, ref, sem).wait()

    def update(it):
        wait_bytes(sums.at[it, 0:n - 1], sum_recv.at[it])
        usable = mrow[...] > 0
        total = [sums[it, 0, place] for place in range(3)]
        for peer in range(1, n):
            for place in range(3):
                total[place] = total[place] + sums[it, peer, place]
        least = jnp.maximum(total[2], LEAST)
        return [jnp.where(usable, total[part] / least, grow[:, part, :]) for part in range(2)], usable

    for it in range(ITERS):
        if it == 0:
            @pl.loop(0, ch)
            def _(k):
                prepare(k)
        else:
            @pl.when(jnp.logical_not(diag))
            def _():
                wait_bytes(xbuf.at[it], x_recv.at[it - 1])
        multiply(it)
        if it == 0:
            pl.semaphore_wait(barrier, n - 1 + (n - 1) * diag.astype(jnp.int32))
        if it < ITERS - 1:
            @pl.when(jnp.logical_not(diag))
            def _():
                sum_to(it, row).start()

            @pl.when(diag)
            def _():
                fresh, usable = update(it)
                for part in range(2):
                    value = fresh[part]
                    if it % 2 == 1:
                        value = jnp.where(usable, 0.5 * (value + old[part]), value)
                    old[part] = value
                    xbuf[it + 1, part] = jnp.where(usable, value, 0.0)
                for step in farthest_first(n):
                    pltpu.make_async_remote_copy(
                        src_ref=xbuf.at[it + 1], dst_ref=xbuf.at[it + 1],
                        send_sem=x_send.at[it], recv_sem=x_recv.at[it],
                        device_id={"row": lax.rem(row + step, n)}, device_id_type=MESH,
                    ).start()
        else:
            for step in farthest_first(n):
                sum_to(it, lax.rem(col + step, n)).start()
            fresh, usable = update(it)
            for part in range(2):
                final[:, part, :] = fresh[part]
            done = pltpu.make_async_copy(final, out, out_sem)
            done.start()
            done.wait()

    for it in range(ITERS - 1):
        @pl.when(jnp.logical_not(diag))
        def _():
            wait_bytes(sums.at[it, 0], sum_send.at[it])

        @pl.when(diag)
        def _():
            wait_bytes(sums.at[0, 0:n - 1, 0:2], x_send.at[it])
    wait_bytes(sums.at[0, 0:n - 1], sum_send.at[ITERS - 1])


def per_device(n, visibility, model, gains_init, antenna_mask):
    assert ITERS % 2 == 1
    ch, _, _, rows, wide = visibility.shape
    f32, bf16 = jnp.float32, jnp.bfloat16
    hbm = pl.BlockSpec(memory_space=pltpu.HBM)
    dma = pltpu.SemaphoreType.DMA
    gains = pl.pallas_call(
        functools.partial(kernel, n),
        out_shape=jax.ShapeDtypeStruct((ch, 2, wide), f32),
        in_specs=[hbm] * 4,
        out_specs=hbm,
        scratch_shapes=[
            pltpu.VMEM((ch, 2, rows, wide), bf16),
            pltpu.VMEM((ch, 2, rows, wide), bf16),
            pltpu.VMEM((ch, rows, 4 * wide), bf16),
            pltpu.VMEM((ch, rows, 2 * wide), bf16),
            pltpu.VMEM((rows, wide), f32),
            pltpu.VMEM((ch, 2, wide), f32),
            pltpu.VMEM((ch, 2, wide), f32),
            pltpu.VMEM((ch, wide), jnp.int32),
            pltpu.VMEM((ch, wide), jnp.int32),
            pltpu.VMEM((2, ch, wide), f32),
            pltpu.VMEM((ITERS, n, 3, ch, wide), f32),
            pltpu.VMEM((ITERS, 2, ch, wide), f32),
            pltpu.VMEM((ch, 2, wide), f32),
            dma((2, ch)),
            dma((4,)),
            dma((ITERS,)),
            dma((ITERS,)),
            dma((ITERS - 1,)),
            dma((ITERS - 1,)),
            dma,
        ],
        compiler_params=pltpu.CompilerParams(
            collective_id=0, has_side_effects=True, vmem_limit_bytes=60 * 2**20
        ),
        cost_estimate=pl.CostEstimate(flops=2 * 48 * 32 * 256 * 256 * 3, bytes_accessed=4 * 2**20, transcendentals=0),
    )(
        visibility.reshape(ch, 2, rows, wide),
        model.reshape(ch, 2, rows, wide),
        gains_init.reshape(ch, 2, gains_init.shape[3]),
        antenna_mask,
    )
    return gains.reshape(ch, 1, 2, wide)


def solution(mesh):
    n = mesh.shape["col"]
    assert mesh.shape["row"] == n
    return jax.shard_map(
        functools.partial(per_device, n),
        mesh=mesh,
        in_specs=(
            P("chan", None, None, "row", "col"),
            P("chan", None, None, "row", "col"),
            P("chan", None, None, None),
            P("chan", None),
        ),
        out_specs=P("chan", None, None, "row"),
        check_vma=False,
    )
```

time: 49.3 us -> 44.7 us (0.907)
  Pallas kernels: 47.7 us -> 43.1 us
    pallas_call x1, Pallas kernels: 47.7 us -> 43.1 us  [per_device(): pl.pallas_call(functools.partial(kernel, n), out_shape=jax.ShapeDtypeStru...]
where the time goes in v2:
time: 44.7 us; the launch traced here: 44.5 us
  Pallas kernels  43.1 us (96%)
  local copies, waits for them, and re-layouts  1.32 us (3%)
    pallas_call x1, Pallas kernels, per_device(): pl.pallas_call(functools.partial(kernel, n), out_shape=jax.ShapeDtypeStru...  43.1 us
    unnamed x1, local copies, waits for them, and re-layouts  1.32 us

profile of v2, /device:TPU:6, one launch (start us, length us, event | category | flops | bytes accessed | tf_op | source)
XLA Modules:
  0.0 44.5 jit_solution(2259461202957676164)
XLA Ops:
  0.0 43.1 %shard_map.46 = f32[8,2,256]{2,1,0:T(2,128)} custom-call(bf16[8,2,256,256]{3,2,1,0:T(8,128)(2,1)} %bitcast.6, bf16[8,2,256,256]{3,2,1,0:T(8,128)(2,1)} %bitcast.7, f32[8,2,2048]{2,1,0:T(2,128)} %bitcast.8, s32[8,2048]{1,0:T(8,128)} %mask.1), custom_call_target="tpu_custom_call" | custom-call | flops 603979776 | bytes 4194304 | tf_op jit(solution)/shard_map/pallas_call | solution.py:215
  43.1 1.3 %copy.7 = f32[8,1,2,256]{3,2,1,0:T(2,128)} copy(f32[8,1,2,256]{3,2,1,0:T(2,128)} %bitcast.9) | data formatting | bytes 32768

commit v3 on v2

v3 whole, which is shorter than its diff:
```python
import functools

import jax
import jax.numpy as jnp
from jax import lax
from jax.experimental import pallas as pl
from jax.experimental.pallas import tpu as pltpu
from jax.sharding import PartitionSpec as P

ITERS = 3
HALVES = 2
CORES = 2
MESH = pl.DeviceIdType.MESH
SHRINK = 2.0**-5
HUGE = 2.0**60
HUGE_SHRINK = 2.0**-65
DEN_LOWER = 2.0**-4
HUGE_GROW = 2.0**126
NUM_LOWER = SHRINK * DEN_LOWER
LEAST = SHRINK * NUM_LOWER
CHUNK = 32


def split(x):
    high = x.astype(jnp.bfloat16).astype(jnp.float32)
    return high, x - high


def stack_bf16(x):
    return jnp.concatenate(split(x), axis=0).astype(jnp.bfloat16)


def dot(x, y, side):
    return lax.dot_general(x, y, (((1,), (side,)), ((), ())), preferred_element_type=jnp.float32)


def farthest_first(n):
    return sorted(range(1, n), key=lambda step: -min(step, n - step))


def kernel(
    n, vis, mod, gin, mask, out,
    vbuf, mbuf, abuf, bbuf, aflip, bflip, weight, gcol, grow, mcol, mrow, old,
    mine, sums, fresh, arrived, last, final,
    in_sem, small_sem, sum_send, sum_recv, x_send, x_recv, last_send, last_recv, out_sem,
):
    chan = lax.axis_index("chan")
    row = lax.axis_index("row")
    col = lax.axis_index("col")
    ch, wide = mcol.shape
    half = ch // HALVES
    core = lax.rem(chan, CORES)
    upper = chan - core + 1
    diag = row == col
    owner = jnp.logical_and(diag, core == 1)
    other = jnp.logical_not(owner)
    column_owner = {"chan": upper, "row": col, "col": col}
    row_owner = {"chan": upper, "row": row, "col": row}

    def loads(k):
        return (
            pltpu.make_async_copy(vis.at[k], vbuf.at[k], in_sem.at[0, k]),
            pltpu.make_async_copy(mod.at[k], mbuf.at[k], in_sem.at[1, k]),
        )

    row_at = pl.ds(pl.multiple_of(row * wide, wide), wide)
    col_at = pl.ds(pl.multiple_of(col * wide, wide), wide)
    small = (
        pltpu.make_async_copy(gin.at[:, :, col_at], gcol, small_sem.at[0]),
        pltpu.make_async_copy(mask.at[:, col_at], mcol, small_sem.at[1]),
        pltpu.make_async_copy(mask.at[:, row_at], mrow, small_sem.at[2]),
        pltpu.make_async_copy(gin.at[:, :, row_at], grow, small_sem.at[3]),
    )
    for k in range(ch):
        for copy in loads(k):
            copy.start()
        if k == 0:
            for copy in small:
                copy.start()

    barrier = pltpu.get_barrier_semaphore()

    def greet(peer):
        pl.semaphore_signal(barrier, inc=1, device_id=peer, device_id_type=MESH)

    for step in range(1, n):
        greet({"col": lax.rem(col + step, n)})
    pl.when(other)(lambda: greet(column_owner))

    @pl.when(owner)
    def _():
        for step in range(n):
            greet({"chan": upper - 1, "col": lax.rem(col + step, n)})

    row_ids = lax.broadcasted_iota(jnp.int32, weight.shape, 0) + row * wide
    col_ids = lax.broadcasted_iota(jnp.int32, weight.shape, 1) + col * wide
    weight[...] = jnp.where(row_ids == col_ids, 0.0, SHRINK).astype(jnp.bfloat16)

    for copy in small:
        copy.wait()

    group = [slice(h * half, (h + 1) * half) for h in range(HALVES)]
    slot = lax.rem(lax.broadcasted_iota(jnp.int32, (2 * half, wide), 0), half)

    def prepare(k):
        for at in range(0, wide, CHUNK):
            rows = pl.ds(at, CHUNK)
            scale = weight[rows]
            m_re = (mbuf[k, 0, rows] * scale).astype(jnp.float32)
            m_im = (mbuf[k, 1, rows] * scale).astype(jnp.float32)
            v_re = vbuf[k, 0, rows].astype(jnp.float32)
            v_im = vbuf[k, 1, rows].astype(jnp.float32)
            values = (m_re * v_re + m_im * v_im, m_re * v_im - m_im * v_re, m_re * m_re + m_im * m_im)
            for place, value in enumerate(values):
                high = value.astype(jnp.bfloat16)
                low = (value - high.astype(jnp.float32)).astype(jnp.bfloat16)
                into, at_lane = (abuf, 2 * place * wide) if place < 2 else (bbuf, 0)
                into[k, rows, at_lane:at_lane + wide] = high
                into[k, rows, at_lane + wide:at_lane + 2 * wide] = low

    def flip():
        @pl.loop(0, ch)
        def _(k):
            for source, target in ((abuf, aflip), (bbuf, bflip)):
                for at in range(0, source.shape[2], wide):
                    target[k, at:at + wide, :] = source[k, :, at:at + wide].T

    def factors(x_re, x_im):
        by_re = stack_bf16(jnp.concatenate([x_re, x_im], axis=0))
        by_im = stack_bf16(jnp.concatenate([-x_im, x_re], axis=0))
        huge = jnp.maximum(jnp.abs(x_re), jnp.abs(x_im)) > HUGE
        down = jnp.where(huge, HUGE_SHRINK, 1.0)
        square = (x_re * down) * (x_re * down) + (x_im * down) * (x_im * down)
        by_b = stack_bf16(jnp.concatenate([jnp.where(huge, 0.0, square), jnp.where(huge, square, 0.0)], axis=0))
        return jnp.concatenate([by_re, by_re, by_im, by_im], axis=1), jnp.concatenate([by_b, by_b], axis=1)

    def add_channel(totals, by, k, flipped):
        num, den = totals
        a, b, side = (aflip, bflip, 0) if flipped else (abuf, bbuf, 1)
        new_num = dot(by[0], a[k], side)
        new_den = dot(by[1], b[k], side)
        here = slot == k % half
        num = jnp.where(here, new_num[0:2 * half] + new_num[2 * half:4 * half], num)
        den = jnp.where(here, new_den[0:2 * half] + new_den[2 * half:4 * half], den)
        return num, den

    def keep(totals, ref):
        num, den = totals
        ref[0] = num[0:half] * NUM_LOWER
        ref[1] = num[half:2 * half] * NUM_LOWER
        ref[2] = den[0:half] * DEN_LOWER + den[half:2 * half] * HUGE_GROW

    def nothing():
        return (jnp.zeros((2 * half, wide), jnp.float32),) * 2

    def quotient(parts):
        total = [parts[0][place] for place in range(3)]
        for part in parts[1:]:
            for place in range(3):
                total[place] = total[place] + part[place]
        least = jnp.maximum(total[2], LEAST)
        return total[0] / least, total[1] / least

    def wait_bytes(ref, sem):
        pltpu.make_async_copy(ref, ref, sem).wait()

    def deliver(it, h, totals):
        if it == ITERS - 1:
            keep(totals, last.at[h, col])
            for step in farthest_first(n):
                pltpu.make_async_remote_copy(
                    src_ref=last.at[h, col], dst_ref=last.at[h, col],
                    send_sem=last_send.at[h], recv_sem=last_recv.at[h],
                    device_id={"col": lax.rem(col + step, n)}, device_id_type=MESH,
                ).start()
            return

        @pl.when(owner)
        def _():
            keep(totals, sums.at[it, h, 1, col])

        @pl.when(other)
        def _():
            keep(totals, mine.at[it, h])
            pltpu.make_async_remote_copy(
                src_ref=mine.at[it, h], dst_ref=sums.at[it, h, core, col],
                send_sem=sum_send.at[it, h], recv_sem=sum_recv.at[it, h, core],
                device_id=row_owner, device_id_type=MESH,
            ).start()

    def settle(it, h, part):
        wait_bytes(sums.at[it, h, part, 0:n - part], sum_recv.at[it, h, part])
        re, im = quotient([sums.at[it, h, part, peer] for peer in range(n)])
        fresh[it, h, part, 0] = re
        fresh[it, h, part, 1] = im
        if part == 1:
            arrived[it, h, 0] = re
            arrived[it, h, 1] = im
        for step in farthest_first(n) + [0] * (part == 0):
            pltpu.make_async_remote_copy(
                src_ref=fresh.at[it, h, part], dst_ref=arrived.at[it, h],
                send_sem=x_send.at[it, h, part], recv_sem=x_recv.at[it, h],
                device_id={"chan": upper - 1 + part, "row": lax.rem(row + step, n)}, device_id_type=MESH,
            ).start()

    def first_factors(h):
        usable = mcol[group[h], :] > 0
        x = [jnp.where(usable, gcol[group[h], part, :], 0.0) for part in range(2)]
        return factors(*x)

    by = [first_factors(h) for h in range(HALVES)]
    totals = nothing()
    for k in range(ch + 1):
        if k < ch:
            for copy in loads(k):
                copy.wait()
        if k > 0:
            totals = add_channel(totals, by[(k - 1) // half], k - 1, False)
        if k < ch:
            prepare(k)
        if k > 0 and k % half == 0:
            if k == half:
                pl.semaphore_wait(barrier, n - 1 + (core == 0).astype(jnp.int32) + (2 * n - 1) * owner.astype(jnp.int32))
            deliver(0, k // half - 1, totals)
            totals = nothing()

    for it in range(ITERS - 1):
        @pl.when(owner)
        def _():
            for h in range(HALVES):
                for part in (1, 0):
                    settle(it, h, part)

        if it == 0:
            flip()
        for h in range(HALVES):
            pl.when(other)(lambda: wait_bytes(arrived.at[it, h], x_recv.at[it, h]))
            usable = mcol[group[h], :] > 0
            x = []
            for part in range(2):
                value = arrived[it, h, part]
                if it % 2 == 1:
                    value = 0.5 * (value + old[h, part])
                elif it + 1 < ITERS - 1:
                    old[h, part] = value
                x.append(jnp.where(usable, value, 0.0))
            by = factors(*x)
            totals = nothing()
            for k in range(h * half, (h + 1) * half):
                totals = add_channel(totals, by, k, True)
            deliver(it + 1, h, totals)

    copies = []
    for h in range(HALVES):
        wait_bytes(last.at[h, 0:n - 1], last_recv.at[h])
        usable = mrow[group[h], :] > 0
        for part, value in enumerate(quotient([last.at[h, peer] for peer in range(n)])):
            final[group[h], part, :] = jnp.where(usable, value, grow[group[h], part, :])
        copies.append(pltpu.make_async_copy(final.at[group[h]], out.at[group[h]], out_sem.at[h]))
        copies[h].start()

    for it in range(ITERS - 1):
        for h in range(HALVES):
            pl.when(other)(lambda: wait_bytes(mine.at[it, h], sum_send.at[it, h]))

            @pl.when(owner)
            def _():
                for part in range(CORES):
                    wait_bytes(sums.at[0, 0, 0, 0:n - part, 0:2], x_send.at[it, h, part])
    for h in range(HALVES):
        wait_bytes(last.at[h, 0:n - 1], last_send.at[h])
    for copy in copies:
        copy.wait()


def per_device(n, visibility, model, gains_init, antenna_mask):
    assert ITERS == 3
    ch, _, _, rows, wide = visibility.shape
    half = ch // HALVES
    f32, bf16 = jnp.float32, jnp.bfloat16
    hbm = pl.BlockSpec(memory_space=pltpu.HBM)
    dma = pltpu.SemaphoreType.DMA
    gains = pl.pallas_call(
        functools.partial(kernel, n),
        out_shape=jax.ShapeDtypeStruct((ch, 2, wide), f32),
        in_specs=[hbm] * 4,
        out_specs=hbm,
        scratch_shapes=[
            pltpu.VMEM((ch, 2, rows, wide), bf16),
            pltpu.VMEM((ch, 2, rows, wide), bf16),
            pltpu.VMEM((ch, rows, 4 * wide), bf16),
            pltpu.VMEM((ch, rows, 2 * wide), bf16),
            pltpu.VMEM((ch, 4 * wide, rows), bf16),
            pltpu.VMEM((ch, 2 * wide, rows), bf16),
            pltpu.VMEM((rows, wide), bf16),
            pltpu.VMEM((ch, 2, wide), f32),
            pltpu.VMEM((ch, 2, wide), f32),
            pltpu.VMEM((ch, wide), jnp.int32),
            pltpu.VMEM((ch, wide), jnp.int32),
            pltpu.VMEM((HALVES, 2, half, wide), f32),
            pltpu.VMEM((ITERS - 1, HALVES, 3, half, wide), f32),
            pltpu.VMEM((ITERS - 1, HALVES, CORES, n, 3, half, wide), f32),
            pltpu.VMEM((ITERS - 1, HALVES, CORES, 2, half, wide), f32),
            pltpu.VMEM((ITERS - 1, HALVES, 2, half, wide), f32),
            pltpu.VMEM((HALVES, n, 3, half, wide), f32),
            pltpu.VMEM((ch, 2, wide), f32),
            dma((2, ch)),
            dma((4,)),
            dma((ITERS - 1, HALVES)),
            dma((ITERS - 1, HALVES, CORES)),
            dma((ITERS - 1, HALVES, CORES)),
            dma((ITERS - 1, HALVES)),
            dma((HALVES,)),
            dma((HALVES,)),
            dma((HALVES,)),
        ],
        compiler_params=pltpu.CompilerParams(
            collective_id=0, has_side_effects=True, vmem_limit_bytes=60 * 2**20
        ),
        cost_estimate=pl.CostEstimate(flops=2 * 48 * 16 * 256 * 256 * 3, bytes_accessed=4 * 2**20, transcendentals=0),
    )(
        visibility.reshape(ch, 2, rows, wide),
        model.reshape(ch, 2, rows, wide),
        gains_init.reshape(ch, 2, gains_init.shape[3]),
        antenna_mask,
    )
    return gains.reshape(ch, 1, 2, wide)


def solution(mesh):
    n = mesh.shape["col"]
    assert mesh.shape["row"] == n and mesh.shape["chan"] % CORES == 0
    return jax.shard_map(
        functools.partial(per_device, n),
        mesh=mesh,
        in_specs=(
            P("chan", None, None, "row", "col"),
            P("chan", None, None, "row", "col"),
            P("chan", None, None, None),
            P("chan", None),
        ),
        out_specs=P("chan", None, None, "row"),
        check_vma=False,
    )
```

time: 44.7 us -> 39.7 us (0.89)
  Pallas kernels: 43.1 us -> 38.1 us
    pallas_call x1, Pallas kernels: 43.1 us -> 38.1 us  [per_device(): pl.pallas_call(functools.partial(kernel, n), out_shape=jax.ShapeDtypeStru...]
where the time goes in v3:
time: 39.7 us; the launch traced here: 39.5 us
  Pallas kernels  38.1 us (96%)
  local copies, waits for them, and re-layouts  1.32 us (3%)
    pallas_call x1, Pallas kernels, per_device(): pl.pallas_call(functools.partial(kernel, n), out_shape=jax.ShapeDtypeStru...  38.1 us
    unnamed x1, local copies, waits for them, and re-layouts  1.32 us

profile of v3, /device:TPU:6, one launch (start us, length us, event | category | flops | bytes accessed | tf_op | source)
XLA Modules:
  0.0 39.5 jit_solution(14397096385782506829)
XLA Ops:
  0.0 38.1 %shard_map.46 = f32[8,2,256]{2,1,0:T(2,128)} custom-call(bf16[8,2,256,256]{3,2,1,0:T(8,128)(2,1)} %bitcast.6, bf16[8,2,256,256]{3,2,1,0:T(8,128)(2,1)} %bitcast.7, f32[8,2,2048]{2,1,0:T(2,128)} %bitcast.8, s32[8,2048]{1,0:T(8,128)} %mask.1), custom_call_target="tpu_custom_call" | custom-call | flops 301989888 | bytes 4194304 | tf_op jit(solution)/shard_map/pallas_call | solution.py:283
  38.1 1.3 %copy.7 = f32[8,1,2,256]{3,2,1,0:T(2,128)} copy(f32[8,1,2,256]{3,2,1,0:T(2,128)} %bitcast.9) | data formatting | bytes 32768

commit v4 on v3

--- a/solution.py
+++ b/solution.py
@@ -71,26 +71,25 @@
         pltpu.make_async_copy(mask.at[:, row_at], mrow, small_sem.at[2]),
         pltpu.make_async_copy(gin.at[:, :, row_at], grow, small_sem.at[3]),
     )
+    barrier = pltpu.get_barrier_semaphore()
+
+    def greet(peer):
+        pl.semaphore_signal(barrier, inc=1, device_id=peer, device_id_type=MESH)
+
+    @pl.when(owner)
+    def _():
+        for step in farthest_first(n) + [0]:
+            for part in range(CORES):
+                if part == 0 or step != 0:
+                    greet({"chan": upper - 1 + part, "col": lax.rem(col + step, n)})
+
     for k in range(ch):
         for copy in loads(k):
             copy.start()
         if k == 0:
             for copy in small:
                 copy.start()
-
-    barrier = pltpu.get_barrier_semaphore()
-
-    def greet(peer):
-        pl.semaphore_signal(barrier, inc=1, device_id=peer, device_id_type=MESH)
-
-    for step in range(1, n):
-        greet({"col": lax.rem(col + step, n)})
-    pl.when(other)(lambda: greet(column_owner))
-
-    @pl.when(owner)
-    def _():
-        for step in range(n):
-            greet({"chan": upper - 1, "col": lax.rem(col + step, n)})
+            pl.when(other)(lambda: greet(column_owner))
 
     row_ids = lax.broadcasted_iota(jnp.int32, weight.shape, 0) + row * wide
     col_ids = lax.broadcasted_iota(jnp.int32, weight.shape, 1) + col * wide
@@ -220,13 +219,15 @@
             prepare(k)
         if k > 0 and k % half == 0:
             if k == half:
-                pl.semaphore_wait(barrier, n - 1 + (core == 0).astype(jnp.int32) + (2 * n - 1) * owner.astype(jnp.int32))
+                pl.when(other)(lambda: pl.semaphore_wait(barrier, 1))
             deliver(0, k // half - 1, totals)
             totals = nothing()
 
     for it in range(ITERS - 1):
         @pl.when(owner)
         def _():
+            if it == 0:
+                pl.semaphore_wait(barrier, CORES * n - 1)
             for h in range(HALVES):
                 for part in (1, 0):
                     settle(it, h, part)
@@ -315,7 +316,7 @@
             dma((HALVES,)),
         ],
         compiler_params=pltpu.CompilerParams(
-            collective_id=0, has_side_effects=True, vmem_limit_bytes=60 * 2**20
+            collective_id=0, has_side_effects=True, vmem_limit_bytes=55184 * 2**10
         ),
         cost_estimate=pl.CostEstimate(flops=2 * 48 * 16 * 256 * 256 * 3, bytes_accessed=4 * 2**20, transcendentals=0),
     )(

time: 39.7 us -> 37.4 us (0.942)
  Pallas kernels: 38.1 us -> 36.7 us
  local copies, waits for them, and re-layouts: 1.32 us -> 0.61 us
    pallas_call x1, Pallas kernels: 38.1 us -> 36.7 us  [per_device(): pl.pallas_call(functools.partial(kernel, n), out_shape=jax.ShapeDtypeStru...]
    unnamed x1, local copies, waits for them, and re-layouts: 1.32 us -> 0.61 us
where the time goes in v4:
time: 37.4 us; the launch traced here: 37.3 us
  Pallas kernels  36.7 us (98%)
  local copies, waits for them, and re-layouts  0.61 us (2%)
    pallas_call x1, Pallas kernels, per_device(): pl.pallas_call(functools.partial(kernel, n), out_shape=jax.ShapeDtypeStru...  36.7 us

profile of v4, /device:TPU:6, one launch (start us, length us, event | category | flops | bytes accessed | tf_op | source)
XLA Modules:
  0.0 37.3 jit_solution(8045523997496074416)
XLA Ops:
  0.0 36.7 %shard_map.46 = f32[8,2,256]{2,1,0:T(2,128)S(1)} custom-call(bf16[8,2,256,256]{3,2,1,0:T(8,128)(2,1)} %bitcast.7, bf16[8,2,256,256]{3,2,1,0:T(8,128)(2,1)} %bitcast.8, f32[8,2,2048]{2,1,0:T(2,128)} %bitcast.9, s32[8,2048]{1,0:T(8,128)} %mask.1), custom_call_target="tpu_custom_call" | custom-call | flops 301989888 | bytes 4194304 | tf_op jit(solution)/shard_map/pallas_call | solution.py:284
  36.7 0.6 %copy.7 = f32[8,1,2,256]{3,2,1,0:T(2,128)} copy(f32[8,1,2,256]{3,2,1,0:T(2,128)S(1)} %bitcast.6) | data formatting | bytes 32768

commit v5 on v4

--- a/solution.py
+++ b/solution.py
@@ -19,6 +19,7 @@
 NUM_LOWER = SHRINK * DEN_LOWER
 LEAST = SHRINK * NUM_LOWER
 CHUNK = 32
+FIRST = 3
 
 
 def split(x):
@@ -41,8 +42,8 @@
 def kernel(
     n, vis, mod, gin, mask, out,
     vbuf, mbuf, abuf, bbuf, aflip, bflip, weight, gcol, grow, mcol, mrow, old,
-    mine, sums, fresh, arrived, last, final,
-    in_sem, small_sem, sum_send, sum_recv, x_send, x_recv, last_send, last_recv, out_sem,
+    mine, sums, fresh, arrived, last,
+    in_sem, small_sem, sum_send, sum_recv, x_send, x_recv, last_send, last_recv,
 ):
     chan = lax.axis_index("chan")
     row = lax.axis_index("row")
@@ -85,7 +86,7 @@
 
     for k in range(ch):
         for copy in loads(k):
-            copy.start()
+            copy.start(priority=int(k >= FIRST))
         if k == 0:
             for copy in small:
                 copy.start()
@@ -94,9 +95,6 @@
     row_ids = lax.broadcasted_iota(jnp.int32, weight.shape, 0) + row * wide
     col_ids = lax.broadcasted_iota(jnp.int32, weight.shape, 1) + col * wide
     weight[...] = jnp.where(row_ids == col_ids, 0.0, SHRINK).astype(jnp.bfloat16)
-
-    for copy in small:
-        copy.wait()
 
     group = [slice(h * half, (h + 1) * half) for h in range(HALVES)]
     slot = lax.rem(lax.broadcasted_iota(jnp.int32, (2 * half, wide), 0), half)
@@ -207,12 +205,19 @@
         x = [jnp.where(usable, gcol[group[h], part, :], 0.0) for part in range(2)]
         return factors(*x)
 
-    by = [first_factors(h) for h in range(HALVES)]
     totals = nothing()
+    ready = 0
     for k in range(ch + 1):
-        if k < ch:
-            for copy in loads(k):
+        if k == ready < ch:
+            until = FIRST if k == 0 else ch
+            for arrival in range(k, until):
+                for copy in loads(arrival):
+                    copy.wait()
+            ready = until
+        if k == 1:
+            for copy in small:
                 copy.wait()
+            by = [first_factors(h) for h in range(HALVES)]
         if k > 0:
             totals = add_channel(totals, by[(k - 1) // half], k - 1, False)
         if k < ch:
@@ -251,14 +256,11 @@
                 totals = add_channel(totals, by, k, True)
             deliver(it + 1, h, totals)
 
-    copies = []
     for h in range(HALVES):
         wait_bytes(last.at[h, 0:n - 1], last_recv.at[h])
         usable = mrow[group[h], :] > 0
         for part, value in enumerate(quotient([last.at[h, peer] for peer in range(n)])):
-            final[group[h], part, :] = jnp.where(usable, value, grow[group[h], part, :])
-        copies.append(pltpu.make_async_copy(final.at[group[h]], out.at[group[h]], out_sem.at[h]))
-        copies[h].start()
+            out[group[h], part, :] = jnp.where(usable, value, grow[group[h], part, :])
 
     for it in range(ITERS - 1):
         for h in range(HALVES):
@@ -270,8 +272,6 @@
                     wait_bytes(sums.at[0, 0, 0, 0:n - part, 0:2], x_send.at[it, h, part])
     for h in range(HALVES):
         wait_bytes(last.at[h, 0:n - 1], last_send.at[h])
-    for copy in copies:
-        copy.wait()
 
 
 def per_device(n, visibility, model, gains_init, antenna_mask):
@@ -285,7 +285,7 @@
         functools.partial(kernel, n),
         out_shape=jax.ShapeDtypeStruct((ch, 2, wide), f32),
         in_specs=[hbm] * 4,
-        out_specs=hbm,
+        out_specs=pl.BlockSpec(memory_space=pltpu.VMEM),
         scratch_shapes=[
             pltpu.VMEM((ch, 2, rows, wide), bf16),
             pltpu.VMEM((ch, 2, rows, wide), bf16),
@@ -304,14 +304,12 @@
             pltpu.VMEM((ITERS - 1, HALVES, CORES, 2, half, wide), f32),
             pltpu.VMEM((ITERS - 1, HALVES, 2, half, wide), f32),
             pltpu.VMEM((HALVES, n, 3, half, wide), f32),
-            pltpu.VMEM((ch, 2, wide), f32),
             dma((2, ch)),
             dma((4,)),
             dma((ITERS - 1, HALVES)),
             dma((ITERS - 1, HALVES, CORES)),
             dma((ITERS - 1, HALVES, CORES)),
             dma((ITERS - 1, HALVES)),
-            dma((HALVES,)),
             dma((HALVES,)),
             dma((HALVES,)),
         ],

time: 37.4 us -> 36.7 us (0.981)
  Pallas kernels: 36.7 us -> 36 us
    pallas_call x1, Pallas kernels: 36.7 us -> 36 us  [per_device(): pl.pallas_call(functools.partial(kernel, n), out_shape=jax.ShapeDtypeStru...]
where the time goes in v5:
time: 36.7 us; the launch traced here: 36.6 us
  Pallas kernels  36 us (98%)
  local copies, waits for them, and re-layouts  0.61 us (2%)
    pallas_call x1, Pallas kernels, per_device(): pl.pallas_call(functools.partial(kernel, n), out_shape=jax.ShapeDtypeStru...  36 us

profile of v5, /device:TPU:6, one launch (start us, length us, event | category | flops | bytes accessed | tf_op | source)
XLA Modules:
  0.0 36.6 jit_solution(11607992122412352911)
XLA Ops:
  0.0 36.0 %shard_map.46 = f32[8,2,256]{2,1,0:T(2,128)S(1)} custom-call(bf16[8,2,256,256]{3,2,1,0:T(8,128)(2,1)} %bitcast.7, bf16[8,2,256,256]{3,2,1,0:T(8,128)(2,1)} %bitcast.8, f32[8,2,2048]{2,1,0:T(2,128)} %bitcast.9, s32[8,2048]{1,0:T(8,128)} %mask.1), custom_call_target="tpu_custom_call" | custom-call | flops 301989888 | bytes 4194304 | tf_op jit(solution)/shard_map/pallas_call | solution.py:284
  36.0 0.6 %copy.7 = f32[8,1,2,256]{3,2,1,0:T(2,128)} copy(f32[8,1,2,256]{3,2,1,0:T(2,128)S(1)} %bitcast.6) | data formatting | bytes 32768

commit v6 on v5

--- a/solution.py
+++ b/solution.py
@@ -10,6 +10,7 @@
 ITERS = 3
 HALVES = 2
 CORES = 2
+DIRECT = ITERS - 2
 MESH = pl.DeviceIdType.MESH
 SHRINK = 2.0**-5
 HUGE = 2.0**60
@@ -39,11 +40,15 @@
     return sorted(range(1, n), key=lambda step: -min(step, n - step))
 
 
+def nearest_to_zero(n):
+    return sorted(range(n), key=lambda place: min(place, n - place))
+
+
 def kernel(
     n, vis, mod, gin, mask, out,
     vbuf, mbuf, abuf, bbuf, aflip, bflip, weight, gcol, grow, mcol, mrow, old,
-    mine, sums, fresh, arrived, last,
-    in_sem, small_sem, sum_send, sum_recv, x_send, x_recv, last_send, last_recv,
+    mine, sums, fresh, arrived, last, direct,
+    in_sem, small_sem, sum_send, sum_recv, x_send, x_recv, last_send, last_recv, direct_send, direct_recv,
 ):
     chan = lax.axis_index("chan")
     row = lax.axis_index("row")
@@ -55,6 +60,8 @@
     diag = row == col
     owner = jnp.logical_and(diag, core == 1)
     other = jnp.logical_not(owner)
+    alone = jnp.logical_and(row == 0, col == 0)
+    distant = 1 - alone.astype(jnp.int32)
     column_owner = {"chan": upper, "row": col, "col": col}
     row_owner = {"chan": upper, "row": row, "col": row}
 
@@ -83,6 +90,11 @@
             for part in range(CORES):
                 if part == 0 or step != 0:
                     greet({"chan": upper - 1 + part, "col": lax.rem(col + step, n)})
+
+    @pl.when(row == 0)
+    def _():
+        for peer in range(n):
+            pl.when(jnp.logical_or(col != 0, peer != 0))(lambda: greet({"row": col, "col": peer}))
 
     for k in range(ch):
         for copy in loads(k):
@@ -164,12 +176,12 @@
     def deliver(it, h, totals):
         if it == ITERS - 1:
             keep(totals, last.at[h, col])
-            for step in farthest_first(n):
-                pltpu.make_async_remote_copy(
+            for peer in nearest_to_zero(n):
+                pl.when(col != peer)(pltpu.make_async_remote_copy(
                     src_ref=last.at[h, col], dst_ref=last.at[h, col],
                     send_sem=last_send.at[h], recv_sem=last_recv.at[h],
-                    device_id={"col": lax.rem(col + step, n)}, device_id_type=MESH,
-                ).start()
+                    device_id={"col": peer}, device_id_type=MESH,
+                ).start)
             return
 
         @pl.when(owner)
@@ -185,6 +197,15 @@
                 device_id=row_owner, device_id_type=MESH,
             ).start()
 
+        if it == DIRECT:
+            pl.when(owner)(lambda: keep(totals, mine.at[it, h]))
+            pl.when(alone)(lambda: keep(totals, direct.at[h, col]))
+            pl.when(jnp.logical_not(alone))(pltpu.make_async_remote_copy(
+                src_ref=mine.at[it, h], dst_ref=direct.at[h, col],
+                send_sem=direct_send.at[h], recv_sem=direct_recv.at[h],
+                device_id={"row": 0, "col": row}, device_id_type=MESH,
+            ).start)
+
     def settle(it, h, part):
         wait_bytes(sums.at[it, h, part, 0:n - part], sum_recv.at[it, h, part])
         re, im = quotient([sums.at[it, h, part, peer] for peer in range(n)])
@@ -193,12 +214,22 @@
         if part == 1:
             arrived[it, h, 0] = re
             arrived[it, h, 1] = im
-        for step in farthest_first(n) + [0] * (part == 0):
+        def send_to(peer):
             pltpu.make_async_remote_copy(
                 src_ref=fresh.at[it, h, part], dst_ref=arrived.at[it, h],
                 send_sem=x_send.at[it, h, part], recv_sem=x_recv.at[it, h],
-                device_id={"chan": upper - 1 + part, "row": lax.rem(row + step, n)}, device_id_type=MESH,
+                device_id={"chan": upper - 1 + part, "row": peer}, device_id_type=MESH,
             ).start()
+
+        if it == DIRECT:
+            for peer in range(1, n):
+                if part == 0:
+                    send_to(peer)
+                else:
+                    pl.when(row != peer)(lambda: send_to(peer))
+        else:
+            for step in farthest_first(n) + [0] * (part == 0):
+                send_to(lax.rem(row + step, n))
 
     def first_factors(h):
         usable = mcol[group[h], :] > 0
@@ -224,7 +255,7 @@
             prepare(k)
         if k > 0 and k % half == 0:
             if k == half:
-                pl.when(other)(lambda: pl.semaphore_wait(barrier, 1))
+                pl.when(other)(lambda: pl.semaphore_wait(barrier, 1 + distant))
             deliver(0, k // half - 1, totals)
             totals = nothing()
 
@@ -232,7 +263,7 @@
         @pl.when(owner)
         def _():
             if it == 0:
-                pl.semaphore_wait(barrier, CORES * n - 1)
+                pl.semaphore_wait(barrier, CORES * n - 1 + distant)
             for h in range(HALVES):
                 for part in (1, 0):
                     settle(it, h, part)
@@ -240,7 +271,17 @@
         if it == 0:
             flip()
         for h in range(HALVES):
-            pl.when(other)(lambda: wait_bytes(arrived.at[it, h], x_recv.at[it, h]))
+            if it == DIRECT:
+                @pl.when(row == 0)
+                def _():
+                    pl.when(col == 0)(lambda: wait_bytes(direct.at[h, 0:n - 1], direct_recv.at[h]))
+                    pl.when(col != 0)(lambda: wait_bytes(direct.at[h], direct_recv.at[h]))
+                    for part, value in enumerate(quotient([direct.at[h, peer] for peer in range(n)])):
+                        arrived[it, h, part] = value
+
+                pl.when(jnp.logical_and(other, row != 0))(lambda: wait_bytes(arrived.at[it, h], x_recv.at[it, h]))
+            else:
+                pl.when(other)(lambda: wait_bytes(arrived.at[it, h], x_recv.at[it, h]))
             usable = mcol[group[h], :] > 0
             x = []
             for part in range(2):
@@ -268,9 +309,16 @@
 
             @pl.when(owner)
             def _():
-                for part in range(CORES):
-                    wait_bytes(sums.at[0, 0, 0, 0:n - part, 0:2], x_send.at[it, h, part])
+                if it == DIRECT:
+                    wait_bytes(sums.at[0, 0, 0, 0:n - 1, 0:2], x_send.at[it, h, 0])
+                    pl.when(row == 0)(lambda: wait_bytes(sums.at[0, 0, 0, 0:n - 1, 0:2], x_send.at[it, h, 1]))
+                    if n > 2:
+                        pl.when(row != 0)(lambda: wait_bytes(sums.at[0, 0, 0, 0:n - 2, 0:2], x_send.at[it, h, 1]))
+                else:
+                    for part in range(CORES):
+                        wait_bytes(sums.at[0, 0, 0, 0:n - part, 0:2], x_send.at[it, h, part])
     for h in range(HALVES):
+        pl.when(jnp.logical_or(row != 0, col != 0))(lambda: wait_bytes(mine.at[0, h], direct_send.at[h]))
         wait_bytes(last.at[h, 0:n - 1], last_send.at[h])
 
 
@@ -304,12 +352,15 @@
             pltpu.VMEM((ITERS - 1, HALVES, CORES, 2, half, wide), f32),
             pltpu.VMEM((ITERS - 1, HALVES, 2, half, wide), f32),
             pltpu.VMEM((HALVES, n, 3, half, wide), f32),
+            pltpu.VMEM((HALVES, n, 3, half, wide), f32),
             dma((2, ch)),
             dma((4,)),
             dma((ITERS - 1, HALVES)),
             dma((ITERS - 1, HALVES, CORES)),
             dma((ITERS - 1, HALVES, CORES)),
             dma((ITERS - 1, HALVES)),
+            dma((HALVES,)),
+            dma((HALVES,)),
             dma((HALVES,)),
             dma((HALVES,)),
         ],

time: 36.7 us -> 34.9 us (0.951)
  Pallas kernels: 36 us -> 34.2 us
    pallas_call x1, Pallas kernels: 36 us -> 34.2 us  [per_device(): pl.pallas_call(functools.partial(kernel, n), out_shape=jax.ShapeDtypeStru...]
where the time goes in v6:
time: 34.9 us; the launch traced here: 34.8 us
  Pallas kernels  34.2 us (98%)
  local copies, waits for them, and re-layouts  0.61 us (2%)
    pallas_call x1, Pallas kernels, per_device(): pl.pallas_call(functools.partial(kernel, n), out_shape=jax.ShapeDtypeStru...  34.2 us

profile of v6, /device:TPU:6, one launch (start us, length us, event | category | flops | bytes accessed | tf_op | source)
XLA Modules:
  0.0 34.8 jit_solution(15553920429439888655)
XLA Ops:
  0.0 34.2 %shard_map.46 = f32[8,2,256]{2,1,0:T(2,128)S(1)} custom-call(bf16[8,2,256,256]{3,2,1,0:T(8,128)(2,1)} %bitcast.7, bf16[8,2,256,256]{3,2,1,0:T(8,128)(2,1)} %bitcast.8, f32[8,2,2048]{2,1,0:T(2,128)} %bitcast.9, s32[8,2048]{1,0:T(8,128)} %mask.1), custom_call_target="tpu_custom_call" | custom-call | flops 301989888 | bytes 4194304 | tf_op jit(solution)/shard_map/pallas_call | solution.py:332
  34.2 0.6 %copy.7 = f32[8,1,2,256]{3,2,1,0:T(2,128)} copy(f32[8,1,2,256]{3,2,1,0:T(2,128)S(1)} %bitcast.6) | data formatting | bytes 32768

commit v7 on v6

--- a/solution.py
+++ b/solution.py
@@ -19,7 +19,7 @@
 HUGE_GROW = 2.0**126
 NUM_LOWER = SHRINK * DEN_LOWER
 LEAST = SHRINK * NUM_LOWER
-CHUNK = 32
+CHUNK = 64
 FIRST = 3
 
 
@@ -41,7 +41,7 @@
 
 
 def nearest_to_zero(n):
-    return sorted(range(n), key=lambda place: min(place, n - place))
+    return sorted(range(n), key=lambda place: (min(place, n - place), -place))
 
 
 def kernel(
@@ -184,27 +184,28 @@
                 ).start)
             return
 
-        @pl.when(owner)
-        def _():
-            keep(totals, sums.at[it, h, 1, col])
-
-        @pl.when(other)
-        def _():
+        if it == DIRECT:
             keep(totals, mine.at[it, h])
-            pltpu.make_async_remote_copy(
-                src_ref=mine.at[it, h], dst_ref=sums.at[it, h, core, col],
-                send_sem=sum_send.at[it, h], recv_sem=sum_recv.at[it, h, core],
-                device_id=row_owner, device_id_type=MESH,
-            ).start()
-
-        if it == DIRECT:
-            pl.when(owner)(lambda: keep(totals, mine.at[it, h]))
             pl.when(alone)(lambda: keep(totals, direct.at[h, col]))
             pl.when(jnp.logical_not(alone))(pltpu.make_async_remote_copy(
                 src_ref=mine.at[it, h], dst_ref=direct.at[h, col],
                 send_sem=direct_send.at[h], recv_sem=direct_recv.at[h],
                 device_id={"row": 0, "col": row}, device_id_type=MESH,
             ).start)
+
+        @pl.when(owner)
+        def _():
+            keep(totals, sums.at[it, h, 1, col])
+
+        @pl.when(other)
+        def _():
+            if it != DIRECT:
+                keep(totals, mine.at[it, h])
+            pltpu.make_async_remote_copy(
+                src_ref=mine.at[it, h], dst_ref=sums.at[it, h, core, col],
+                send_sem=sum_send.at[it, h], recv_sem=sum_recv.at[it, h, core],
+                device_id=row_owner, device_id_type=MESH,
+            ).start()
 
     def settle(it, h, part):
         wait_bytes(sums.at[it, h, part, 0:n - part], sum_recv.at[it, h, part])

time: 34.9 us -> 34.8 us (level)
  no operation moved by 1% of the time
where the time goes in v7:
time: 34.8 us; the launch traced here: 34.7 us
  Pallas kernels  34.1 us (98%)
  local copies, waits for them, and re-layouts  0.61 us (2%)
    pallas_call x1, Pallas kernels, per_device(): pl.pallas_call(functools.partial(kernel, n), out_shape=jax.ShapeDtypeStru...  34.1 us

profile of v7, /device:TPU:6, one launch (start us, length us, event | category | flops | bytes accessed | tf_op | source)
XLA Modules:
  0.0 34.7 jit_solution(79264733887168488)
XLA Ops:
  0.0 34.1 %shard_map.46 = f32[8,2,256]{2,1,0:T(2,128)S(1)} custom-call(bf16[8,2,256,256]{3,2,1,0:T(8,128)(2,1)} %bitcast.7, bf16[8,2,256,256]{3,2,1,0:T(8,128)(2,1)} %bitcast.8, f32[8,2,2048]{2,1,0:T(2,128)} %bitcast.9, s32[8,2048]{1,0:T(8,128)} %mask.1), custom_call_target="tpu_custom_call" | custom-call | flops 301989888 | bytes 4194304 | tf_op jit(solution)/shard_map/pallas_call | solution.py:333
  34.1 0.6 %copy.7 = f32[8,1,2,256]{3,2,1,0:T(2,128)} copy(f32[8,1,2,256]{3,2,1,0:T(2,128)S(1)} %bitcast.6) | data formatting | bytes 32768

commit v8 on v7

--- a/solution.py
+++ b/solution.py
@@ -163,12 +163,11 @@
         return (jnp.zeros((2 * half, wide), jnp.float32),) * 2
 
     def quotient(parts):
-        total = [parts[0][place] for place in range(3)]
-        for part in parts[1:]:
-            for place in range(3):
-                total[place] = total[place] + part[place]
-        least = jnp.maximum(total[2], LEAST)
-        return total[0] / least, total[1] / least
+        total = [[part[place] for part in parts] for place in range(3)]
+        while len(total[0]) > 1:
+            total = [[one + two for one, two in zip(terms[::2], terms[1::2])] for terms in total]
+        scale = 1.0 / jnp.maximum(total[2][0], LEAST)
+        return total[0][0] * scale, total[1][0] * scale
 
     def wait_bytes(ref, sem):
         pltpu.make_async_copy(ref, ref, sem).wait()

time: 34.8 us -> 34.8 us (level)
  no operation moved by 1% of the time
where the time goes in v8:
time: 34.8 us; the launch traced here: 34.7 us
  Pallas kernels  34.1 us (98%)
  local copies, waits for them, and re-layouts  0.61 us (2%)
    pallas_call x1, Pallas kernels, per_device(): pl.pallas_call(functools.partial(kernel, n), out_shape=jax.ShapeDtypeStru...  34.1 us

profile of v8, /device:TPU:6, one launch (start us, length us, event | category | flops | bytes accessed | tf_op | source)
XLA Modules:
  0.0 34.7 jit_solution(1210199113288874365)
XLA Ops:
  0.0 34.1 %shard_map.46 = f32[8,2,256]{2,1,0:T(2,128)S(1)} custom-call(bf16[8,2,256,256]{3,2,1,0:T(8,128)(2,1)} %bitcast.7, bf16[8,2,256,256]{3,2,1,0:T(8,128)(2,1)} %bitcast.8, f32[8,2,2048]{2,1,0:T(2,128)} %bitcast.9, s32[8,2048]{1,0:T(8,128)} %mask.1), custom_call_target="tpu_custom_call" | custom-call | flops 301989888 | bytes 4194304 | tf_op jit(solution)/shard_map/pallas_call | solution.py:332
  34.1 0.6 %copy.7 = f32[8,1,2,256]{3,2,1,0:T(2,128)} copy(f32[8,1,2,256]{3,2,1,0:T(2,128)S(1)} %bitcast.6) | data formatting | bytes 32768
